TPU v7x, 128 devices: a whole 4x4x4 slice. The times are simulated.
128 devices in a mesh: dp: 8 (over y_hi, x), width: 4 (over y_lo, core), heads: 4 (over z).
Axes of the slice: x: 4, y: 4 (y_hi: 2, y_lo: 2; y = y_hi * 2 + y_lo), z: 4, core: 2. Of those that a mesh axis runs over, the one named last changes fastest.
Arguments:
- tokens: bfloat16 [16384, 1280], P(('dp', 'heads'), 'width'), may hold values from -22 to 22
- ln_gain: float32 [2, 1280], P(None, 'width'), may hold values from 0.5 to 1.5
- ln_bias: float32 [2, 1280], P(None, 'width'), may hold values from -4 to 4
- w_attn: bfloat16 [3, 1280, 1280], P(None, 'width', 'heads'), may hold values from -0.15625 to 0.15625
- b_qv: float32 [2, 1280], P(None, 'heads'), may hold values from -4 to 4
- w_proj: bfloat16 [1280, 1280], P('heads', 'width'), may hold values from -1.25 to 1.25
- b_proj: float32 [1280], P('width'), may hold values from -4 to 4
- w_fc: bfloat16 [1280, 5120], P('width', 'heads'), may hold values from -1 to 1
- b_fc: float32 [5120], P('heads'), may hold values from -4 to 4
- w_out: bfloat16 [5120, 1280], P('heads', 'width'), may hold values from -0.078125 to 0.078125
- b_out: float32 [1280], P('width'), may hold values from -4 to 4
- d_out: bfloat16 [16384, 1280], P(('dp', 'heads'), 'width'), may hold values from -22 to 22
Outputs:
- block_out: bfloat16 [16384, 1280], P(('dp', 'heads'), 'width')
- d_tokens: bfloat16 [16384, 1280], P(('dp', 'heads'), 'width')
- d_ln_gain: float32 [2, 1280], P(None, 'width')
- d_ln_bias: float32 [2, 1280], P(None, 'width')
- d_w_attn: float32 [3, 1280, 1280], P(None, 'width', 'heads')
- d_b_qv: float32 [2, 1280], P(None, 'heads')
- d_w_proj: float32 [1280, 1280], P('heads', 'width')
- d_b_proj: float32 [1280], P('width')
- d_w_fc: float32 [1280, 5120], P('width', 'heads')
- d_b_fc: float32 [5120], P('heads')
- d_w_out: float32 [5120, 1280], P('heads', 'width')
- d_b_out: float32 [1280], P('width')
All inputs are finite; a program needn't handle non-finite values.
Results may differ from a plain program's by a relative error of at most 0.023.
Values may be sent and summed in bfloat16 or wider, within the bound.
A program may use at most 192 MiB of HBM per device.

v0:
```python
import functools

import jax
import jax.numpy as jnp
from jax import lax
from jax.experimental import pallas as pl
from jax.experimental.pallas import tpu as pltpu
from jax.sharding import PartitionSpec as P

F32, BF16 = jnp.float32, jnp.bfloat16
D, HS, ROWS, PART, QUARTER, HEADS = 1280, 64, 128, 320, 512, 5
PAIR = 2 * PART
STRIP = PART // 4
HALF = ROWS // 2
EPSILON = 1e-05
GELU_COEF = 0.7978845608028654
MASKED = -1e30
VMEM = pl.BlockSpec(memory_space=pltpu.VMEM)
ANY = pl.BlockSpec(memory_space=pl.ANY)
TILES = D // 256


def nn(a, b):
    return jnp.dot(a, b, preferred_element_type=F32)


def nt(a, b):
    return lax.dot_general(a, b, (((1,), (1,)), ((), ())), preferred_element_type=F32)


def tn(a, b):
    return lax.dot_general(a, b, (((0,), (0,)), ((), ())), preferred_element_type=F32)


def rows_of(start, size=ROWS):
    return pl.ds(pl.multiple_of(start, size), size)


def block_of(who):
    return pl.ds(pl.multiple_of(who * PART, 64), PART)


def tile_of(i, size):
    return pl.ds(pl.multiple_of(i * size, size), size)


def sub_block(quarter, w):
    return w + lax.rem(quarter, 2) * (3 - 2 * w)


class Place:
    def __init__(self):
        self.dp, self.w, self.h = (lax.axis_index(n) for n in ("dp", "width", "heads"))
        self.x = lax.rem(self.dp, 4)
        self.wc = self.w + 1 - 2 * lax.rem(self.w, 2)
        self.wy = lax.rem(self.w + 2, 4)
        self.wyc = lax.rem(self.wc + 2, 4)
        across = lax.rem(self.dp + 4, 8)
        self.core = (self.dp, self.wc, self.h)
        self.near = (self.dp, self.wy, self.h)
        self.near_core = (self.dp, self.wyc, self.h)
        self.far = (across, self.wy, self.h)
        self.opposite = (across, self.w, self.h)
        self.width_peers = ((self.near, self.wy), (self.near_core, self.wyc), (self.core, self.wc))

        beyond = lax.rem(self.dp + 4, 8) - self.x
        self.dp_peers = [self.along_x(k) for k in (1, 2, 3)] + [self.opposite]
        self.dp_peers += [(beyond + lax.rem(self.x + k, 4), self.w, self.h) for k in (1, 2, 3)]

    def along_z(self, k):
        return (self.dp, self.w, lax.rem(self.h + k, 4))

    def along_x(self, k):
        return (self.dp - self.x + lax.rem(self.x + k, 4), self.w, self.h)

    def chunk(self, k):
        return lax.rem(self.h + k, 4)


def greet(devices):
    barrier = pltpu.get_barrier_semaphore()
    for device in devices:
        pl.semaphore_signal(barrier, inc=1, device_id=device, device_id_type=pl.DeviceIdType.MESH)
    pl.semaphore_wait(barrier, len(devices))


class Move:
    def __init__(self, copy):
        self.copy, self.left = copy, False
        self.start, self.wait_recv = copy.start, copy.wait_recv

    def wait_send(self):
        if not self.left:
            self.copy.wait_send()
        self.left = True

    def wait(self):
        self.wait_recv()
        self.wait_send()


class Links:
    def __init__(self, sent, landed):
        self.sent, self.landed, self.copies, self.count = sent, landed, [], 0

    def reserve(self, count):
        self.count += count
        return self.count - count

    def make(self, i, source, target, device):
        return pltpu.make_async_remote_copy(
            src_ref=source,
            dst_ref=target,
            send_sem=self.sent.at[i],
            recv_sem=self.landed.at[i],
            device_id=device,
            device_id_type=pl.DeviceIdType.MESH,
        )

    def plan(self, source, target, device):
        self.copies.append(Move(self.make(self.reserve(1), source, target, device)))
        return self.copies[-1]

    def send(self, source, target, device):
        copy = self.plan(source, target, device)
        copy.start()
        return copy


class GatherZ:
    def __init__(self, links, at, rows):
        right, left = at.along_z(1), at.along_z(3)
        own, ahead, behind = (rows.at[pl.ds(i * ROWS, ROWS)] for i in range(3))
        self.right = links.send(own, behind, right)
        self.left = links.send(own, ahead, left)
        self.low = links.plan(
            rows.at[pl.ds(2 * ROWS, HALF)], rows.at[pl.ds(3 * ROWS, HALF)], right
        )
        self.high = links.plan(
            rows.at[pl.ds(ROWS + HALF, HALF)], rows.at[pl.ds(3 * ROWS + HALF, HALF)], left
        )

    def neighbours(self):
        self.left.wait_recv()
        self.high.start()
        self.right.wait_recv()
        self.low.start()

    def rest(self):
        self.low.wait_recv()
        self.high.wait_recv()


class SumZ:
    def __init__(self, links, at, stage, parts, over):
        self.stage, self.parts, self.over = stage, parts, over
        right, left = at.along_z(1), at.along_z(3)
        top, bottom = pl.ds(0, HALF), pl.ds(HALF, HALF)
        self.far_right = links.plan(stage.at[3, top], over.at[0], right)
        self.far_left = links.plan(stage.at[3, bottom], over.at[1], left)
        self.right_bottom = links.plan(stage.at[1, bottom], parts.at[0, bottom], right)
        self.right_top = links.plan(stage.at[1, top], parts.at[0, top], right)
        self.left_top = links.plan(stage.at[2, top], parts.at[1, top], left)
        self.left_bottom = links.plan(stage.at[2, bottom], parts.at[1, bottom], left)

    def sent(self):
        for copy in (self.far_right, self.far_left, self.right_bottom, self.right_top, self.left_top, self.left_bottom):
            copy.wait_send()

    def send_across(self):
        self.far_right.start()
        self.far_left.start()

    def send_near(self):
        self.right_bottom.start()
        self.left_top.start()

    def join_ahead(self):
        self.far_right.wait_recv()
        joined = self.stage[1, 0:HALF, :].astype(F32) + self.over[0].astype(F32)
        self.stage[1, 0:HALF, :] = joined.astype(BF16)
        self.right_top.start()

    def join_behind(self):
        self.far_left.wait_recv()
        joined = self.stage[2, HALF:, :].astype(F32) + self.over[1].astype(F32)
        self.stage[2, HALF:, :] = joined.astype(BF16)
        self.left_bottom.start()

    def result(self):
        for copy in (self.right_bottom, self.right_top, self.left_top, self.left_bottom):
            copy.wait_recv()
        return self.stage[0].astype(F32) + self.parts[0].astype(F32) + self.parts[1].astype(F32)


class GradientSum:
    def __init__(self, links, at, grad, columns, pair, strips, cross, final):
        self.links, self.at, self.grad, self.columns = links, at, grad, columns
        self.pair, self.strips, self.cross, self.final = pair, strips, cross, final
        self.strip = rows_of(at.x * STRIP, STRIP)
        self.total = [pair.at[0, self.strip], pair.at[1, self.strip]]

    def mine(self, who):
        return self.grad.at[block_of(who), self.columns]

    def send_core(self):
        at, links = self.at, self.links
        self.core = [
            links.send(self.mine(at.wc), self.pair.at[0], at.core),
            links.send(self.mine(at.wyc), self.pair.at[1], at.core),
        ]

    def sent_core(self):
        for copy in self.core:
            copy.wait_send()

    def add_core(self):
        for i, who in ((0, self.at.w), (1, self.at.wy)):
            self.core[i].wait_recv()
            self.pair[i] = (self.pair[i].astype(F32) + self.mine(who)[...].astype(F32)).astype(BF16)

    def send_x(self):
        at, links = self.at, self.links
        self.add_core()
        self.along = [
            links.send(
                self.pair.at[:, rows_of(lax.rem(at.x + k, 4) * STRIP, STRIP)], self.strips.at[k - 1], at.along_x(k)
            )
            for k in (2, 1, 3)
        ]

    def send_x_by_neighbours(self):
        at, links = self.at, self.links
        self.add_core()
        right, left = at.along_x(1), at.along_x(3)
        ahead, across, behind = (rows_of(lax.rem(at.x + k, 4) * STRIP, STRIP) for k in (1, 2, 3))
        parts, over = self.strips, self.strips.at[2]
        self.over_x = [
            links.send(self.pair.at[0, across], over.at[0], right),
            links.send(self.pair.at[1, across], over.at[1], left),
        ]
        self.along = [
            links.send(self.pair.at[1, ahead], parts.at[0, 1], right),
            links.send(self.pair.at[0, behind], parts.at[1, 0], left),
            links.plan(self.pair.at[0, ahead], parts.at[0, 0], right),
            links.plan(self.pair.at[1, behind], parts.at[1, 1], left),
        ]
        self.relayed = (self.pair.at[0, ahead], self.pair.at[1, behind])

    def relay_x(self):
        for i in range(2):
            self.over_x[i].wait_recv()
            joined = self.relayed[i][...].astype(F32) + self.strips[2, i].astype(F32)
            self.relayed[i][...] = joined.astype(BF16)
            self.along[2 + i].start()

    def add_strips(self):
        for copy in self.along:
            copy.wait_recv()
        for i in range(2):
            joined = self.total[i][...].astype(F32)
            for k in range(3 if len(self.along) == 3 else 2):
                joined = joined + self.strips[k, i].astype(F32)
            self.total[i][...] = joined.astype(BF16)

    def send_y(self):
        self.add_strips()
        self.over = [
            self.links.send(self.total[1], self.cross.at[0], self.at.near),
            self.links.send(self.total[1], self.cross.at[1], self.at.far),
            self.links.send(self.total[0], self.cross.at[2], self.at.opposite),
        ]

    def send_far(self):
        self.add_strips()
        self.over = [self.links.send(self.total[1], self.cross.at[0], self.at.far)]

    def send_opposite(self):
        self.over[0].wait()
        joined = self.total[0][...].astype(F32) + self.cross[0].astype(F32)
        self.total[0][...] = joined.astype(BF16)
        self.over = [self.links.send(self.total[0], self.cross.at[1], self.at.opposite)]

    def send_back(self, passing):
        at, links = self.at, self.links
        joined = self.total[0][...].astype(F32)
        for copy in self.over:
            copy.wait()
        places = (0, 1, 2) if len(self.over) == 3 else (1,)
        for place in places:
            joined = joined + self.cross[place].astype(F32)
        self.total[0][...] = joined.astype(BF16)
        strip = self.final.at[self.strip]
        self.back = [links.send(self.total[0], strip, at.along_x(k)) for k in ((1, 3) if passing else (2, 1, 3))]
        self.passing = passing
        return strip

    def pass_back(self):
        at, links = self.at, self.links
        behind, ahead = lax.rem(at.x + 3, 4) * STRIP, lax.rem(at.x + 1, 4) * STRIP
        first = self.final.at[pl.ds(pl.multiple_of(behind, 16), 48)]
        second = self.final.at[pl.ds(pl.multiple_of(ahead + 48, 16), 32)]
        self.back[0].wait_recv()
        self.back[1].wait_recv()
        self.back = [
            links.send(first, first, at.along_x(1)),
            links.send(second, second, at.along_x(3)),
        ]

    def finish(self):
        for copy in self.back:
            copy.wait_recv()


class GradientSumY:
    def __init__(self, links, at, grad, pair, cross, strips, half, final):
        self.links, self.at, self.grad = links, at, grad
        self.pair, self.cross, self.strips, self.half, self.final = pair, cross, strips, half, final
        part = at.dp // 4
        self.kept = pl.ds(pl.multiple_of(part * PAIR, PAIR), PAIR)
        self.given = pl.ds(pl.multiple_of((1 - part) * PAIR, PAIR), PAIR)
        self.strip = rows_of(at.x * STRIP, STRIP)

    def mine(self, who):
        return self.grad.at[block_of(who)]

    def send_core(self):
        at, links = self.at, self.links
        self.core = [
            links.send(self.mine(at.wc), self.pair.at[0], at.core),
            links.send(self.mine(at.wyc), self.pair.at[1], at.core),
        ]

    def send_y(self):
        at, links = self.at, self.links
        for i, who in ((0, at.w), (1, at.wy)):
            self.core[i].wait_recv()
            self.pair[i] = (self.pair[i].astype(F32) + self.mine(who)[...].astype(F32)).astype(BF16)
        self.over = [
            links.send(self.pair.at[1, :, self.kept], self.cross.at[0], at.near),
            links.send(self.pair.at[1, :, self.given], self.cross.at[1], at.far),
            links.send(self.pair.at[0, :, self.given], self.cross.at[2], at.opposite),
        ]

    def send_x(self):
        at, links = self.at, self.links
        joined = self.pair[0, :, self.kept].astype(F32)
        for k in range(3):
            self.over[k].wait_recv()
            joined = joined + self.cross[k].astype(F32)
        self.pair[0, :, self.kept] = joined.astype(BF16)
        self.along = [
            links.send(
                self.pair.at[0, rows_of(lax.rem(at.x + k, 4) * STRIP, STRIP), self.kept],
                self.strips.at[k - 1],
                at.along_x(k),
            )
            for k in (2, 1, 3)
        ]

    def send_back(self):
        at, links = self.at, self.links
        joined = self.pair[0, self.strip, self.kept].astype(F32)
        for copy in self.along:
            copy.wait_recv()
        for k in range(3):
            joined = joined + self.strips[k].astype(F32)
        self.half[self.strip, :] = joined.astype(BF16)
        place = self.half.at[self.strip]
        self.back = [links.send(place, place, at.along_x(k)) for k in (2, 1, 3)]

    def send_opposite(self, sem):
        for copy in self.back:
            copy.wait_recv()
        place = self.final.at[:, self.kept]
        self.last = self.links.send(self.half, place, self.at.opposite)
        keep = pltpu.make_async_copy(self.half, place, sem)
        keep.start()
        return keep

    def finish(self):
        self.last.wait_recv()


def norm_stats(values):
    mean = jnp.mean(values, axis=1, keepdims=True)
    centred = values - mean
    scale = lax.rsqrt(jnp.mean(centred * centred, axis=1, keepdims=True) + EPSILON)
    return centred * scale, scale


def norm_gradient(grad, unit, scale, gain):
    scaled = grad * gain
    mean = jnp.mean(scaled, axis=1, keepdims=True)
    along = jnp.mean(scaled * unit, axis=1, keepdims=True)
    return scale * (scaled - mean - unit * along)


def interleave(first, second):
    pieces = []
    for head in range(HEADS):
        part = slice(head * HS, (head + 1) * HS)
        pieces += [first[:, part], second[:, part]]
    return jnp.concatenate(pieces, axis=1)


def mask_last(scores, quarter, shift):
    shape = (4, ROWS, ROWS)
    owner = lax.broadcasted_iota(jnp.int32, shape, 0)
    if quarter % 2:
        owner = 3 - owner
    key = owner * ROWS + lax.broadcasted_iota(jnp.int32, shape, 1)
    query = lax.broadcasted_iota(jnp.int32, shape, 2) + shift
    seen = (key <= query).reshape(QUARTER, ROWS)
    parts = [scores[:, i * ROWS : (i + 1) * ROWS] for i in range(scores.shape[1] // ROWS)]
    parts = [jnp.where(seen, part, MASKED) for part in parts]
    return parts[0] if len(parts) == 1 else jnp.concatenate(parts, axis=1)


def column_sum(values):
    return jnp.sum(values, axis=0, keepdims=True)


SCRATCH = dict(
    wkv=((D, PAIR), BF16),
    wq=((D, PART), BF16),
    wpt=((D, PART), BF16),
    wf=((D, D), BF16),
    wt=((D, D), BF16),
    wa_raw=((3, PART, PART), BF16),
    wp_raw=((PART, PART), BF16),
    xa=((D, ROWS), BF16),
    da=((D, ROWS), BF16),
    vl=((8, PART), F32),
    vg=((4, 8, PART), F32),
    vec=((8, D), F32),
    bf=((8, D), F32),
    x=((ROWS, D), BF16),
    x1=((QUARTER, D), BF16),
    q=((QUARTER, PAIR), BF16),
    kv=((4, 4, ROWS, PAIR), BF16),
    kvt=((PAIR, 2048), BF16),
    att=((QUARTER, PART), BF16),
    att_t=((4, PART, ROWS), F32),
    lse=((32, 128), F32),
    delta=((32, 128), F32),
    middle=((ROWS, D), F32),
    stage=((4, ROWS, D), BF16),
    parts=((2, ROWS, D), BF16),
    over=((2, HALF, D), BF16),
    d_all=((QUARTER, D), BF16),
    x2=((QUARTER, D), BF16),
    hidden_grad=((QUARTER, D), F32),
    hid=((QUARTER, D), BF16),
    gp=((QUARTER, D), BF16),
    stage_g=((4, ROWS, D), BF16),
    parts_g=((3, ROWS, D), BF16),
    parts_b=((2, ROWS, D), BF16),
    over_b=((2, HALF, D), BF16),
    gm=((ROWS, D), F32),
    grad_f=((D, D), BF16),
    grad_t=((D, D), BF16),
    pair_f=((2, PART, D), BF16),
    pair_t=((2, PART, D), BF16),
    pair_q=((2, PART, PAIR), BF16),
    pair_k=((2, PART, PAIR), BF16),
    strips_f=((3, STRIP, PAIR), BF16),
    half_f=((PART, PAIR), BF16),
    strips_t=((3, 2, STRIP, D), BF16),
    strips_q=((3, 2, STRIP, PAIR), BF16),
    strips_k=((3, 2, STRIP, PAIR), BF16),
    cross_f=((3, PART, PAIR), BF16),
    cross_t=((3, STRIP, D), BF16),
    cross_q=((3, STRIP, PAIR), BF16),
    cross_k=((3, STRIP, PAIR), BF16),
    g_all=((QUARTER, D), BF16),
    go=((QUARTER, PAIR), BF16),
    dkv=((HEADS, 4, 4, ROWS, 128), BF16),
    take=((2, HEADS, 4, ROWS, 128), BF16),
    take_y=((HEADS, 4, ROWS, 128), BF16),
    dq=((QUARTER, PART), BF16),
    gkv=((QUARTER, PAIR), BF16),
    sums=((16, D), F32),
    sums_n=((8, PART), F32),
    sums_z=((3, 8, PART), F32),
    sums_w=((4, 8, PART), F32),
    take_w=((3, 8, PART), F32),
    take_v=((3, 8, D), F32),
    sums_d=((8, D), F32),
    sums_x=((7, 8, D), F32),
)
COPIES = 176


def block_kernel(*refs):
    names = ("tok", "dout", "gain", "shift", "b_proj", "b_out", "wa_in", "bqv", "wp_in", "wf_in", "b_fc", "wo_in")
    names += ("bo", "dt", "fin_f", "fin_t", "fin_q", "fin_k", "fin_v")
    names += tuple(SCRATCH) + ("sent", "landed", "local")
    r = dict(zip(names, refs))
    (tok, dout, gain, shift, b_proj, b_out, wa_in, bqv, wp_in, wf_in, b_fc, wo_in) = refs[:12]
    (bo, dt, fin_f, fin_t, fin_q, fin_k, fin_v) = refs[12:19]
    at = Place()
    w, h = at.w, at.h
    links = Links(r["sent"], r["landed"])
    local = r["local"]
    mine = sub_block(h, w)
    vec = r["vec"]

    wf, wt = r["wf"], r["wt"]
    loads = [
        pltpu.make_async_copy(wa_in, r["wa_raw"], local.at[0]),
        pltpu.make_async_copy(wp_in, r["wp_raw"], local.at[1]),
        pltpu.make_async_copy(wo_in, wt.at[block_of(w)], local.at[2]),
        pltpu.make_async_copy(wf_in, wf.at[block_of(w)], local.at[3]),
        pltpu.make_async_copy(tok.at[:, rows_of(mine * ROWS)], r["xa"].at[block_of(w)], local.at[4]),
        pltpu.make_async_copy(dout.at[:, rows_of(mine * ROWS)], r["da"].at[block_of(w)], local.at[5]),
    ]
    for copy in loads:
        copy.start()
    vl = r["vl"]
    vl[0:2, :] = gain[...]
    vl[2:4, :] = shift[...]
    vl[4:5, :] = b_proj[...].reshape(1, PART)
    vl[5:6, :] = b_out[...].reshape(1, PART)
    vl[6:8, :] = jnp.zeros((2, PART), F32)
    r["bf"][0:1, :] = b_fc[...].reshape(1, D)
    greet(
        [at.core, at.near, at.near_core, at.far, at.opposite]
        + [at.along_z(k) for k in (1, 2, 3)]
        + [at.along_x(k) for k in (1, 2, 3)]
        + [device for device in at.dp_peers[4:]]
    )

    def spread(source, slots):
        return [
            links.send(source.at[:, rows_of(sub_block(h, peer) * ROWS)], slots.at[block_of(w)], device)
            for device, peer in at.width_peers
        ]

    arrive = spread(tok, r["xa"])
    arrive += [links.send(vl, r["vg"].at[w], device) for device, _ in at.width_peers]
    r["vg"][w] = vl[...]

    class Weight:
        def __init__(self, full, device):
            own_block, next_block = full.at[block_of(w)], full.at[block_of(at.wy)]
            self.over = links.send(own_block, own_block, device)
            self.core = links.send(own_block, own_block, at.core)
            self.other = links.plan(next_block, next_block, at.core)

        def forward(self):
            self.over.wait_recv()
            self.other.start()

        def ready(self):
            self.core.wait_recv()
            self.other.wait_recv()

    loads[0].wait()
    r["wkv"][block_of(w), :] = interleave(r["wa_raw"][1], r["wa_raw"][2])
    weight_kv = Weight(r["wkv"], at.far)
    r["wq"][block_of(w), :] = r["wa_raw"][0]
    weight_q = Weight(r["wq"], at.far)
    loads[1].wait()
    r["wpt"][block_of(w), :] = r["wp_raw"][...].T
    loads[4].wait()
    for copy in arrive:
        copy.wait_recv()

    arrive_d = spread(dout, r["da"])
    vec[...] = jnp.concatenate([r["vg"][i] for i in range(4)], axis=1)
    r["x"][...] = r["xa"][...].T
    unit, _ = norm_stats(r["x"][...].astype(F32))
    x1, kv, q = r["x1"], r["kv"], r["q"]
    x1[0:ROWS, :] = (unit * vec[0:1, :] + vec[2:3, :]).astype(BF16)
    gather = GatherZ(links, at, x1)
    value_bias = interleave(jnp.zeros((1, PART), F32), bqv[1:2, :])
    weight_kv.forward()
    weight_kv.ready()
    weight_p = Weight(r["wpt"], at.far)
    loads[2].wait()
    weight_t = Weight(wt, at.far)
    quarter = [at.chunk(k) for k in (0, 1, 3, 2)]
    shares, passed = [], []

    def key_rows(first, count):
        rows = (nn(x1[first * ROWS : (first + count) * ROWS, :], r["wkv"][...]) + value_bias).astype(BF16)
        for i in range(count):
            block = kv.at[quarter[first + i], w]
            block[...] = rows[i * ROWS : (i + 1) * ROWS, :]
            shares.append(links.send(block, block, at.near))
            shares.append(links.send(block, block, at.core))

    def pass_on(i):
        shares[2 * i].wait_recv()
        block = kv.at[quarter[i], at.wy]
        passed.append(links.send(block, block, at.core))

    key_rows(0, 1)
    gather.neighbours()
    key_rows(1, 2)
    weight_q.forward()
    pass_on(0)
    gather.rest()
    d_all = r["d_all"]
    loads[5].wait()
    for copy in arrive_d:
        copy.wait_recv()
    d_all[0:ROWS, :] = r["da"][...].T
    gather_d = GatherZ(links, at, d_all)
    key_rows(3, 1)
    weight_q.ready()
    queries = (nn(x1[...], r["wq"][...]) + bqv[0:1, :]).astype(BF16).astype(F32) * HS**-0.5
    q[...] = interleave(queries.astype(BF16), jnp.zeros((QUARTER, PART), BF16))
    weight_p.forward()
    for i in (1, 2, 3):
        pass_on(i)
    loads[3].wait()
    weight_f = Weight(wf, at.near)
    for i in range(4):
        shares[2 * i + 1].wait_recv()
        passed[i].wait_recv()

    kvt, att, att_t, lse = r["kvt"], r["att"], r["att_t"], r["lse"]

    def keys_of(j, lanes):
        return kv[j, :, :, lanes].reshape(QUARTER, lanes.stop - lanes.start)

    for j in range(4):
        for head in range(HEADS):
            tile = slice(head * 128, (head + 1) * 128)
            kvt[tile, j * QUARTER : (j + 1) * QUARTER] = keys_of(j, tile).T
    stage = r["stage"]
    sum_p = SumZ(links, at, stage, r["parts"], r["over"])

    def attend_chunk(j, slot):
        shift = sub_block(j, w) * ROWS
        apart = jnp.zeros((ROWS, 128), BF16)
        for first, count in ((0, 2), (2, 2), (4, 1)):
            lanes = slice(first * 128, (first + count) * 128)
            query = q[rows_of(slot * ROWS), lanes]
            if count == 2:
                top = jnp.concatenate([query[:, :128], apart], axis=1)
                query = jnp.concatenate([top, jnp.concatenate([apart, query[:, 128:]], axis=1)], axis=0)
            scores = [nt(keys_of(b, lanes), query) for b in range(j + 1)]
            scores[j] = mask_last(scores[j], j, shift)
            peak = functools.reduce(jnp.maximum, [jnp.max(s, axis=0, keepdims=True) for s in scores])
            total, result = 0.0, 0.0
            for b in range(j + 1):
                weights = jnp.exp(scores[b] - peak)
                total = total + column_sum(weights)
                result = result + nn(kvt[lanes, b * QUARTER : (b + 1) * QUARTER], weights.astype(BF16))
            inverse, log_total = 1.0 / total, peak + jnp.log(total)
            for i in range(count):
                head, part = first + i, slice(i * 128, (i + 1) * 128)
                values = result[i * 128 + HS : (i + 1) * 128, part]
                att_t[slot, head * HS : (head + 1) * HS, :] = values * inverse[:, part]
                lse[pl.ds(slot * 8 + head, 1), :] = log_total[:, part]

    gather_d.neighbours()
    weight_p.ready()

    @pl.loop(0, 4)
    def _(i):
        slot = jnp.where(i == 0, 3, jnp.where(i == 3, 0, i))
        j = at.chunk(jnp.where(slot == 3, 2, jnp.where(slot == 2, 3, slot)))
        for case in range(4):
            pl.when(j == case)(functools.partial(attend_chunk, case, slot))
        attended = att_t[slot].T.astype(BF16)
        att[rows_of(slot * ROWS), :] = attended
        stage[slot] = nt(attended, r["wpt"][...]).astype(BF16)
        pl.when(i == 0)(sum_p.send_across)
        pl.when(i == 1)(sum_p.right_bottom.start)
        pl.when(i == 1)(weight_t.forward)
        pl.when(i == 2)(sum_p.left_top.start)
        pl.when(i == 2)(sum_p.join_ahead)
        pl.when(i == 2)(sum_p.join_behind)

    gather_d.rest()
    weight_t.ready()
    weight_f.forward()
    middle = r["x"][...].astype(F32) + vec[4:5, :] + sum_p.result()
    r["middle"][...] = middle
    unit, _ = norm_stats(middle)
    x2, hid, gp = r["x2"], r["hid"], r["gp"]
    x2[0:ROWS, :] = (unit * vec[1:2, :] + vec[3:4, :]).astype(BF16)

    gather = GatherZ(links, at, x2)
    hidden_grad = r["hidden_grad"]
    for t in range(TILES):
        tile = slice(t * 256, (t + 1) * 256)
        hidden_grad[:, tile] = nn(d_all[...], wt[:, tile])
    weight_f.ready()
    stage_g, parts_g = r["stage_g"], r["parts_g"]
    moves = []

    def feed(first, count):
        rows = slice(first * ROWS, (first + count) * ROWS)

        for t in range(TILES):
            tile = slice(t * 256, (t + 1) * 256)
            u = nn(x2[rows, :], wf[:, tile]) + r["bf"][0:1, tile]
            square = u * u
            th = jnp.tanh(GELU_COEF * (u + 0.044715 * square * u))
            hid[rows, tile] = (0.5 * u * (1.0 + th)).astype(BF16)
            slope = 0.5 * (1.0 + th) + 0.5 * u * (1.0 - th * th) * (GELU_COEF * (1.0 + 0.134145 * square))
            gp[rows, tile] = (hidden_grad[rows, tile] * slope).astype(BF16)
        for t in range(TILES):
            tile = slice(t * 256, (t + 1) * 256)
            product = nt(gp[rows, :], wf[tile, :]).astype(BF16)
            for i in range(count):
                stage_g[first + i, :, tile] = product[i * ROWS : (i + 1) * ROWS]
        for i in range(first, first + count):
            if i:
                moves.append(links.send(stage_g.at[i], parts_g.at[i - 1], at.along_z((0, 1, 3, 2)[i])))

    feed(0, 1)
    gather.neighbours()
    feed(1, 2)
    gather.rest()
    feed(3, 1)
    grad_f, grad_t = r["grad_f"], r["grad_t"]

    def gradient_sum(tag, grad, columns, final):
        return GradientSum(
            links, at, grad, columns, r["pair_" + tag], r["strips_" + tag], r["cross_" + tag], final
        )

    @pl.loop(0, TILES)
    def _(t):
        grad_t[tile_of(t, 256), :] = tn(d_all[:, tile_of(t, 256)], hid[...]).astype(BF16)

    whole = slice(0, D)
    sum_t = gradient_sum("t", grad_t, whole, fin_t)
    sum_t.send_core()

    @pl.loop(0, TILES)
    def _(t):
        grad_f[tile_of(t, 256), :] = tn(x2[:, tile_of(t, 256)], gp[...]).astype(BF16)

    sum_f = GradientSumY(links, at, grad_f, r["pair_f"], r["cross_f"], r["strips_f"], r["half_f"], fin_f)
    sum_f.send_core()
    sum_t.send_x_by_neighbours()
    unit, scale = norm_stats(r["middle"][...])
    grad = d_all[0:ROWS, :].astype(F32)
    grad_normed = stage_g[0].astype(F32)
    for i in range(3):
        moves[i].wait_recv()
        grad_normed = grad_normed + parts_g[i].astype(F32)
    grad_middle = grad + norm_gradient(grad_normed, unit, scale, vec[1:2, :])
    r["gm"][...] = grad_middle
    branch = grad_middle.astype(BF16)
    g_all = r["g_all"]
    g_all[0:ROWS, :] = branch
    gather = GatherZ(links, at, g_all)
    sums = r["sums"]
    sums[1:2, :] = column_sum(grad_normed * unit)
    sums[3:4, :] = column_sum(grad_normed)
    sums[4:5, :] = column_sum(grad)
    sums[5:6, :] = column_sum(branch.astype(F32))
    sums[8:9, :] = column_sum(gp[...].astype(F32))
    sum_f.send_y()
    sum_p.sent()
    sum_b = SumZ(links, at, stage, r["parts_b"], r["over_b"])

    @pl.loop(0, TILES)
    def _(t):
        product = nt(hid[...], wt[tile_of(t, 256), :]).astype(BF16)
        for i in range(4):
            stage[i, :, tile_of(t, 256)] = product[i * ROWS : (i + 1) * ROWS]


    dkv, go, dq, dq_t, delta = r["dkv"], r["go"], r["dq"], att_t, r["delta"]
    take, take_y, gkv = r["take"], r["take_y"], r["gkv"]
    dkv[...] = jnp.zeros(dkv.shape, BF16)

    def rows_back(first, count):
        rows = slice(first * ROWS, (first + count) * ROWS)
        grad = nn(g_all[rows, :], r["wpt"][...]).astype(BF16)
        go[rows, :] = interleave(jnp.zeros((count * ROWS, PART), BF16), grad)
        for i in range(count):
            slot = first + i
            both = grad[i * ROWS : (i + 1) * ROWS, :].astype(F32).T * att_t[slot]
            delta[slot * 8 : slot * 8 + HEADS, :] = jnp.sum(both.reshape(HEADS, HS, ROWS), axis=1)

    shared = links.reserve(3 * HEADS)

    def head_move(kind, head):
        source = dkv.at[head, :, (at.wyc, at.wc, at.wy)[kind]]
        target = take_y.at[head] if kind == 2 else take.at[1 - kind, head]
        return links.make(shared + kind * HEADS + head, source, target, at.near if kind == 2 else at.core)

    def cross_head(head):
        head_move(0, head).wait_recv()
        for j in range(4):
            both = dkv[head, j, at.wy].astype(F32) + take[1, head, j].astype(F32)
            dkv[head, j, at.wy] = both.astype(BF16)
        head_move(2, head).start()

    def back_chunk(j, slot):
        rows = rows_of(slot * ROWS)

        @pl.loop(0, HEADS)
        def _(head):
            tile = tile_of(head, 128)
            side = jnp.concatenate([q[rows, tile], go[rows, tile]], axis=0)
            log_total = lse[pl.ds(slot * 8 + head, 1), :]
            inner = delta[pl.ds(slot * 8 + head, 1), :]
            grads = []
            for b in range(j + 1):
                products = nt(kv[b, :, :, tile].reshape(QUARTER, 128), side)
                scores = products[:, :128]
                if b == j:
                    scores = mask_last(scores, j, sub_block(j, w) * ROWS)
                probs = jnp.exp(scores - log_total)
                grads.append((probs * (products[:, 128:] - inner)).astype(BF16))
                both = nn(jnp.concatenate([grads[b], probs.astype(BF16)], axis=1), side)
                both = dkv[head, b].reshape(QUARTER, 128).astype(F32) + both
                dkv[head, b] = both.astype(BF16).reshape(4, ROWS, 128)
            result = nn(kvt[tile, 0 : (j + 1) * QUARTER], jnp.concatenate(grads, axis=0))
            dq_t[slot, tile_of(head, HS), :] = result[:HS, :] * HS**-0.5
            pl.when(slot == 3)(lambda: head_move(0, head).start())

    def near_back():
        gather.neighbours()
        rows_back(1, 2)

    for copy in moves:
        copy.wait_send()
    rows_back(0, 1)

    sum_t.relay_x()

    def far_back():
        gather.rest()
        rows_back(3, 1)
        sum_b.send_across()
        sum_b.send_near()

    @pl.loop(0, 4)
    def _(slot):
        pl.when(slot == 1)(near_back)
        pl.when(slot == 3)(far_back)
        j = at.chunk(jnp.where(slot == 2, 3, jnp.where(slot == 3, 2, slot)))
        for case in range(4):
            pl.when(j == case)(functools.partial(back_chunk, case, slot))

    for slot in range(4):
        dq[slot * ROWS : (slot + 1) * ROWS, :] = dq_t[slot].T.astype(BF16)
    for head in range(HEADS):
        cross_head(head)
    for head in range(HEADS):
        head_move(1, head).start()
    sum_f.send_x()
    slots = []
    for j in range(4):
        k = lax.rem(j + 4 - h, 4)
        slots.append(jnp.where(k == 2, 3, jnp.where(k == 3, 2, k)))
    keep = []

    def send_back(total, passing=False):
        strip = total.send_back(passing)
        copy = pltpu.make_async_copy(total.total[0], strip, local.at[7 + len(keep)])
        copy.start()
        keep.append(copy)

    def send_rows(back, target):
        place = target.at[:, rows_of(mine * ROWS)]
        keep = pltpu.make_async_copy(back.at[block_of(w)], place, local.at[6])
        keep.start()
        copies = [links.send(back.at[block_of(peer)], place, device) for device, peer in at.width_peers]
        keep.wait()
        return copies

    sum_t.sent_core()

    @pl.loop(0, TILES)
    def _(t):
        tile = tile_of(t, 256)
        pieces = [tn(x1[:, tile], dq[...]).astype(BF16), tn(g_all[:, tile], att[...]).astype(BF16)]
        grad_t[tile, PAIR:] = jnp.concatenate(pieces, axis=1)

    sum_q = gradient_sum("q", grad_t, slice(PAIR, D), fin_q)
    sum_q.send_core()
    sum_t.send_far()
    sums[9:10, 0:PART] = column_sum(dq[...].astype(F32))
    sum_b.join_ahead()
    sum_b.join_behind()
    sum_q.send_x()
    sum_f.send_back()
    result = r["middle"][...] + vec[5:6, :] + sum_b.result()
    r["xa"][...] = result.astype(BF16).T
    returns = send_rows(r["xa"], bo)

    for head in range(HEADS):
        tile = slice(head * 128, (head + 1) * 128)
        head_move(1, head).wait_recv()
        head_move(2, head).wait_recv()
        for j in range(4):
            total = dkv[head, j, w].astype(F32) + take[0, head, j].astype(F32) + take_y[head, j].astype(F32)
            gkv[rows_of(slots[j] * ROWS), tile] = total.astype(BF16)


    @pl.loop(0, TILES)
    def _(t):
        tile = tile_of(t, 256)
        grad_t[tile, 0:PAIR] = tn(x1[:, tile], gkv[...]).astype(BF16)

    sum_k = gradient_sum("k", grad_t, slice(0, PAIR), fin_k)
    sum_k.send_core()
    sum_t.send_opposite()
    sum_b.sent()
    sum_l = SumZ(links, at, stage, r["parts"], r["over"])

    def first_partial(first, count):
        rows = slice(first * ROWS, (first + count) * ROWS)
        product = (nt(dq[rows, :], r["wq"][...]) + nt(gkv[rows, :], r["wkv"][...])).astype(BF16)
        for i in range(count):
            stage[first + i] = product[i * ROWS : (i + 1) * ROWS]

    first_partial(3, 1)
    sum_l.send_across()
    first_partial(1, 2)
    sum_l.send_near()
    grad_values = column_sum(gkv[...].astype(F32))
    for head in range(HEADS):
        sums[9:10, PART + head * HS : PART + (head + 1) * HS] = grad_values[:, head * 128 + HS : (head + 1) * 128]
    sums[9:10, PAIR:] = jnp.zeros((1, PAIR), F32)
    sums[10:16, :] = jnp.zeros((6, D), F32)
    sums[6:8, :] = jnp.zeros((2, D), F32)
    over_v = [links.send(sums.at[8:16], r["take_v"].at[i], at.width_peers[i][0]) for i in range(3)]
    sum_k.send_x()
    keep.append(sum_f.send_opposite(local.at[7 + len(keep)]))
    sum_l.join_ahead()
    sum_l.join_behind()
    first_partial(0, 1)
    sum_q.send_y()
    send_back(sum_t, True)
    grad_normed = sum_l.result()
    unit, scale = norm_stats(r["x"][...].astype(F32))
    sums[0:1, :] = column_sum(grad_normed * unit)
    sums[2:3, :] = column_sum(grad_normed)
    for part in range(4):
        r["sums_w"][part] = sums[0:8, part * PART : (part + 1) * PART]
    over_w = [
        links.send(r["sums_w"].at[peer], r["take_w"].at[i], device)
        for i, (device, peer) in enumerate(at.width_peers)
    ]
    result = r["gm"][...] + norm_gradient(grad_normed, unit, scale, vec[0:1, :])
    r["da"][...] = result.astype(BF16).T
    returns += send_rows(r["da"], dt)
    sum_t.pass_back()
    send_back(sum_q)

    for copy in over_w + over_v:
        copy.wait_recv()
    sums_d = r["sums_d"]
    normed = r["sums_w"][w] + r["take_w"][0] + r["take_w"][1] + r["take_w"][2]
    biases = sums[8:10, :] + r["take_v"][0, 0:2] + r["take_v"][1, 0:2] + r["take_v"][2, 0:2]
    r["sums_n"][...] = normed
    over_z = [links.send(r["sums_n"], r["sums_z"].at[k - 1], at.along_z(k)) for k in (1, 2, 3)]
    sum_k.send_y()
    for copy in over_z:
        copy.wait_recv()
    normed = r["sums_n"][...] + r["sums_z"][0] + r["sums_z"][1] + r["sums_z"][2]
    sums_d[...] = jnp.zeros((8, D), F32)
    for i in range(6):
        sums_d[i // 3 : i // 3 + 1, (i % 3) * 384 : (i % 3) * 384 + PART] = normed[i : i + 1, :]
    sums_d[2:4, :] = biases
    over_x = [links.send(sums_d, r["sums_x"].at[i], device) for i, device in enumerate(at.dp_peers)]
    send_back(sum_k)
    total = sums_d[...]
    for i, copy in enumerate(over_x):
        copy.wait_recv()
        total = total + r["sums_x"][i]
    fin_v[...] = total
    for copy in keep:
        copy.wait()
    for total in (sum_t, sum_f, sum_q, sum_k):
        total.finish()
    for copy in returns:
        copy.wait()
    for kind in range(3):
        for head in range(HEADS):
            head_move(kind, head).wait_send()
    for copy in links.copies:
        copy.wait_send()


def block(*inputs):
    return pl.pallas_call(
        block_kernel,
        name="block",
        out_shape=(
            jax.ShapeDtypeStruct((PART, QUARTER), BF16),
            jax.ShapeDtypeStruct((PART, QUARTER), BF16),
            jax.ShapeDtypeStruct((PART, D), BF16),
            jax.ShapeDtypeStruct((PART, D), BF16),
            jax.ShapeDtypeStruct((PART, PAIR), BF16),
            jax.ShapeDtypeStruct((PART, PAIR), BF16),
            jax.ShapeDtypeStruct((8, D), F32),
        ),
        in_specs=[ANY, ANY, VMEM, VMEM, VMEM, VMEM, ANY, VMEM, ANY, ANY, VMEM, ANY],
        out_specs=(ANY, ANY, ANY, ANY, ANY, ANY, VMEM),
        scratch_shapes=[pltpu.VMEM(shape, kind) for shape, kind in SCRATCH.values()]
        + [pltpu.SemaphoreType.DMA((COPIES,)), pltpu.SemaphoreType.DMA((COPIES,)), pltpu.SemaphoreType.DMA((12,))],
        compiler_params=pltpu.CompilerParams(collective_id=1, has_side_effects=True, vmem_limit_bytes=64 * 2**20),
    )(*inputs)


def finish_kernel(*refs):
    inputs, outputs, (f, t, qp, kv, d_wa, d_wp, d_wf, d_wo, rows_b, rows_d, sems) = refs[:7], refs[7:19], refs[19:]
    bo, dt, f_in, t_in, qp_in, kv_in, v = inputs
    out, d_tok, gain, shift, wa_out, d_bqv, wp_out, d_bp, wf_out, d_bf, wo_out, d_bo = outputs
    loads = [
        pltpu.make_async_copy(source, target, sems.at[i])
        for i, (source, target) in enumerate(((t_in, t), (f_in, f), (qp_in, qp), (kv_in, kv), (bo, rows_b), (dt, rows_d)))
    ]
    stores = [
        pltpu.make_async_copy(source, target, sems.at[6 + i])
        for i, (source, target) in enumerate(
            ((rows_b, out), (rows_d, d_tok), (d_wo, wo_out), (d_wf, wf_out), (d_wa, wa_out), (d_wp, wp_out))
        )
    ]
    for copy in loads:
        copy.start()
    loads[0].wait()
    d_wo[...] = t[...].astype(F32)
    stores[2].start()
    loads[1].wait()
    d_wf[...] = f[...].astype(F32)
    stores[3].start()
    loads[2].wait()
    d_wa[0] = qp[:, :PART].astype(F32)
    d_wp[...] = qp[:, PART:].astype(F32).T
    stores[5].start()
    loads[3].wait()
    both = kv[...].astype(F32)
    d_wa[1] = jnp.concatenate([both[:, head * 128 : head * 128 + HS] for head in range(HEADS)], axis=1)
    d_wa[2] = jnp.concatenate([both[:, head * 128 + HS : (head + 1) * 128] for head in range(HEADS)], axis=1)
    stores[4].start()
    for i in range(2):
        loads[4 + i].wait()
        stores[i].start()
    rows = [v[i // 3 : i // 3 + 1, (i % 3) * 384 : (i % 3) * 384 + PART] for i in range(6)]
    gain[0:1, :] = rows[0]
    gain[1:2, :] = rows[1]
    shift[0:1, :] = rows[2]
    shift[1:2, :] = rows[3]
    d_bo[...] = rows[4].reshape(PART)
    d_bp[...] = rows[5].reshape(PART)
    d_bf[...] = v[2:3, :].reshape(D)
    d_bqv[0:1, :] = v[3:4, 0:PART]
    d_bqv[1:2, :] = v[3:4, PART:PAIR]
    for copy in stores:
        copy.wait()


def finish(*inputs):
    shapes = [
        ((PART, QUARTER), BF16),
        ((PART, QUARTER), BF16),
        ((2, PART), F32),
        ((2, PART), F32),
        ((3, PART, PART), F32),
        ((2, PART), F32),
        ((PART, PART), F32),
        ((PART,), F32),
        ((PART, D), F32),
        ((D,), F32),
        ((PART, D), F32),
        ((PART,), F32),
    ]
    return pl.pallas_call(
        finish_kernel,
        name="finish",
        out_shape=[jax.ShapeDtypeStruct(shape, kind) for shape, kind in shapes],
        in_specs=[ANY] * 6 + [VMEM],
        out_specs=[ANY, ANY, VMEM, VMEM, ANY, VMEM, ANY, VMEM, ANY, VMEM, ANY, VMEM],
        scratch_shapes=[
            pltpu.VMEM((PART, D), BF16),
            pltpu.VMEM((PART, D), BF16),
            pltpu.VMEM((PART, PAIR), BF16),
            pltpu.VMEM((PART, PAIR), BF16),
            pltpu.VMEM((3, PART, PART), F32),
            pltpu.VMEM((PART, PART), F32),
            pltpu.VMEM((PART, D), F32),
            pltpu.VMEM((PART, D), F32),
            pltpu.VMEM((PART, QUARTER), BF16),
            pltpu.VMEM((PART, QUARTER), BF16),
            pltpu.SemaphoreType.DMA((12,)),
        ],
        compiler_params=pltpu.CompilerParams(vmem_limit_bytes=63 * 2**20),
    )(*inputs)


def shards(tokens, ln_gain, ln_bias, w_attn, b_qv, w_proj, b_proj, w_fc, b_fc, w_out, b_out, d_out):
    parts = block(tokens.T, d_out.T, ln_gain, ln_bias, b_proj, b_out, w_attn, b_qv, w_proj, w_fc, b_fc, w_out.T)
    results = list(finish(*parts))
    for i in (0, 1, 10):
        results[i] = results[i].T
    return tuple(results)


def solution(mesh):
    in_specs = (
        P(("dp", "heads"), "width"),
        P(None, "width"),
        P(None, "width"),
        P(None, "width", "heads"),
        P(None, "heads"),
        P("heads", "width"),
        P("width"),
        P("width", "heads"),
        P("heads"),
        P("heads", "width"),
        P("width"),
        P(("dp", "heads"), "width"),
    )
    out_specs = (
        P(("dp", "heads"), "width"),
        P(("dp", "heads"), "width"),
        P(None, "width"),
        P(None, "width"),
        P(None, "width", "heads"),
        P(None, "heads"),
        P("heads", "width"),
        P("width"),
        P("width", "heads"),
        P("heads"),
        P("heads", "width"),
        P("width"),
    )
    return jax.shard_map(shards, mesh=mesh, in_specs=in_specs, out_specs=out_specs, check_vma=False)
```

profile of v0, /device:TPU:0, one launch (start us, length us, event | category | flops | bytes accessed | tf_op | source)
XLA Modules:
  0.0 174.3 jit_solution(9411678308398354605)
XLA Ops:
  0.6 168.1 %block.1 = (bf16[320,512]{1,0:T(8,128)(2,1)}, bf16[320,512]{1,0:T(8,128)(2,1)}, bf16[320,1280]{1,0:T(8,128)(2,1)}, bf16[320,1280]{1,0:T(8,128)(2,1)}, bf16[320,6...) custom-call(bf16[320,512]{1,0:T(8,128)(2,1)} %bitcast.7, bf16[320,512]{1,0:T(8,128)(2,1)} %bitcast.8, ...), custom_call_target="tpu_custom_call" | custom-call | tf_op jit(solution)/shard_map/block/pallas_call | solution.py:991
  168.8 5.3 %finish.1 = (bf16[320,512]{1,0:T(8,128)(2,1)}, bf16[320,512]{1,0:T(8,128)(2,1)}, f32[2,320]{1,0:T(2,128)}, f32[2,320]{1,0:T(2,128)}, f32[3,320,320]{2,1,0:T(8,12...) custom-call(bf16[320,512]{1,0:T(8,128)(2,1)} %get-tuple-element.31.r, ...), custom_call_target="tpu_custom_call" | custom-call | tf_op jit(solution)/shard_map/finish/pallas_call | solution.py:1074
where the time goes:
time: 176 us; the launch traced here: 174 us
  Pallas kernels  173 us (98%)
    pallas_call x1, Pallas kernels, block(): pl.pallas_call(block_kernel, name='block', out_shape=(jax.ShapeDtypeStruc...  168 us
    pallas_call x1, Pallas kernels, finish(): pl.pallas_call(finish_kernel, name='finish', out_shape=[jax.ShapeDtypeStr...  5.31 us

commit v1 on v0

--- a/solution.py
+++ b/solution.py
@@ -404,14 +404,14 @@
     return jnp.concatenate(pieces, axis=1)
 
 
-def mask_last(scores, quarter, shift):
-    shape = (4, ROWS, ROWS)
-    owner = lax.broadcasted_iota(jnp.int32, shape, 0)
+def mask_last(scores, quarter, shift, start=0):
+    shape = (scores.shape[0] // ROWS, ROWS, ROWS)
+    owner = start + lax.broadcasted_iota(jnp.int32, shape, 0)
     if quarter % 2:
         owner = 3 - owner
     key = owner * ROWS + lax.broadcasted_iota(jnp.int32, shape, 1)
     query = lax.broadcasted_iota(jnp.int32, shape, 2) + shift
-    seen = (key <= query).reshape(QUARTER, ROWS)
+    seen = (key <= query).reshape(scores.shape[0], ROWS)
     parts = [scores[:, i * ROWS : (i + 1) * ROWS] for i in range(scores.shape[1] // ROWS)]
     parts = [jnp.where(seen, part, MASKED) for part in parts]
     return parts[0] if len(parts) == 1 else jnp.concatenate(parts, axis=1)
@@ -591,10 +591,13 @@
             shares.append(links.send(block, block, at.near))
             shares.append(links.send(block, block, at.core))
 
+    for i in range(4):
+        block = kv.at[quarter[i], at.wy]
+        passed.append(links.plan(block, block, at.core))
+
     def pass_on(i):
         shares[2 * i].wait_recv()
-        block = kv.at[quarter[i], at.wy]
-        passed.append(links.send(block, block, at.core))
+        passed[i].start()
 
     key_rows(0, 1)
     gather.neighbours()
@@ -613,27 +616,26 @@
     queries = (nn(x1[...], r["wq"][...]) + bqv[0:1, :]).astype(BF16).astype(F32) * HS**-0.5
     q[...] = interleave(queries.astype(BF16), jnp.zeros((QUARTER, PART), BF16))
     weight_p.forward()
-    for i in (1, 2, 3):
-        pass_on(i)
-    loads[3].wait()
-    weight_f = Weight(wf, at.near)
     for i in range(4):
         shares[2 * i + 1].wait_recv()
-        passed[i].wait_recv()
-
-    kvt, att, att_t, lse = r["kvt"], r["att"], r["att_t"], r["lse"]
-
-    def keys_of(j, lanes):
-        return kv[j, :, :, lanes].reshape(QUARTER, lanes.stop - lanes.start)
-
-    for j in range(4):
-        for head in range(HEADS):
-            tile = slice(head * 128, (head + 1) * 128)
-            kvt[tile, j * QUARTER : (j + 1) * QUARTER] = keys_of(j, tile).T
-    stage = r["stage"]
-    sum_p = SumZ(links, at, stage, r["parts"], r["over"])
-
-    def attend_chunk(j, slot):
+
+    kvt, att, att_t, lse, delta = r["kvt"], r["att"], r["att_t"], r["lse"], r["delta"]
+    here = w - lax.rem(w, 2)
+    there = 2 - here
+
+    def half_keys(j, lanes, start):
+        return kv[j, pl.ds(start, 2), :, lanes].reshape(2 * ROWS, lanes.stop - lanes.start)
+
+    def half_columns(j, start):
+        return pl.ds(pl.multiple_of(j * QUARTER + start * ROWS, 2 * ROWS), 2 * ROWS)
+
+    def transpose_keys(start):
+        for j in range(4):
+            for head in range(HEADS):
+                tile = slice(head * 128, (head + 1) * 128)
+                kvt[tile, half_columns(j, start)] = half_keys(j, tile, start).T
+
+    def attend_chunk(j, slot, start, merge):
         shift = sub_block(j, w) * ROWS
         apart = jnp.zeros((ROWS, 128), BF16)
         for first, count in ((0, 2), (2, 2), (4, 1)):
@@ -642,20 +644,51 @@
             if count == 2:
                 top = jnp.concatenate([query[:, :128], apart], axis=1)
                 query = jnp.concatenate([top, jnp.concatenate([apart, query[:, 128:]], axis=1)], axis=0)
-            scores = [nt(keys_of(b, lanes), query) for b in range(j + 1)]
-            scores[j] = mask_last(scores[j], j, shift)
+            scores = [nt(half_keys(b, lanes, start), query) for b in range(j + 1)]
+            scores[j] = mask_last(scores[j], j, shift, start)
             peak = functools.reduce(jnp.maximum, [jnp.max(s, axis=0, keepdims=True) for s in scores])
             total, result = 0.0, 0.0
+            if merge:
+                rows = [pl.ds(slot * 8 + first + i, 1) for i in range(count)]
+                before = jnp.concatenate([lse[row, :] for row in rows], axis=1)
+                peak = jnp.maximum(peak, before)
+                scale = jnp.exp(before - peak)
+                total = jnp.concatenate([delta[row, :] for row in rows], axis=1) * scale
             for b in range(j + 1):
                 weights = jnp.exp(scores[b] - peak)
                 total = total + column_sum(weights)
-                result = result + nn(kvt[lanes, b * QUARTER : (b + 1) * QUARTER], weights.astype(BF16))
-            inverse, log_total = 1.0 / total, peak + jnp.log(total)
+                result = result + nn(kvt[lanes, half_columns(b, start)], weights.astype(BF16))
             for i in range(count):
                 head, part = first + i, slice(i * 128, (i + 1) * 128)
+                place, row = slice(head * HS, (head + 1) * HS), pl.ds(slot * 8 + head, 1)
                 values = result[i * 128 + HS : (i + 1) * 128, part]
-                att_t[slot, head * HS : (head + 1) * HS, :] = values * inverse[:, part]
-                lse[pl.ds(slot * 8 + head, 1), :] = log_total[:, part]
+                if merge:
+                    values = (values + att_t[slot, place, :] * scale[:, part]) * (1.0 / total[:, part])
+                    lse[row, :] = peak[:, part] + jnp.log(total[:, part])
+                else:
+                    lse[row, :] = peak[:, part]
+                    delta[row, :] = total[:, part]
+                att_t[slot, place, :] = values
+
+    transpose_keys(here)
+
+    @pl.loop(0, 4)
+    def _(slot):
+        pl.when(slot == 1)(functools.partial(pass_on, 1))
+        pl.when(slot == 3)(functools.partial(pass_on, 2))
+        j = at.chunk(jnp.where(slot == 3, 2, jnp.where(slot == 2, 3, slot)))
+        for case in range(4):
+            pl.when(j == case)(functools.partial(attend_chunk, case, slot, here, False))
+
+    pass_on(3)
+    loads[3].wait()
+    weight_f = Weight(wf, at.near)
+    for i in range(4):
+        passed[i].wait_recv()
+
+    transpose_keys(there)
+    stage = r["stage"]
+    sum_p = SumZ(links, at, stage, r["parts"], r["over"])
 
     gather_d.neighbours()
     weight_p.ready()
@@ -665,7 +698,7 @@
         slot = jnp.where(i == 0, 3, jnp.where(i == 3, 0, i))
         j = at.chunk(jnp.where(slot == 3, 2, jnp.where(slot == 2, 3, slot)))
         for case in range(4):
-            pl.when(j == case)(functools.partial(attend_chunk, case, slot))
+            pl.when(j == case)(functools.partial(attend_chunk, case, slot, there, True))
         attended = att_t[slot].T.astype(BF16)
         att[rows_of(slot * ROWS), :] = attended
         stage[slot] = nt(attended, r["wpt"][...]).astype(BF16)
@@ -770,7 +803,7 @@
             stage[i, :, tile_of(t, 256)] = product[i * ROWS : (i + 1) * ROWS]
 
 
-    dkv, go, dq, dq_t, delta = r["dkv"], r["go"], r["dq"], att_t, r["delta"]
+    dkv, go, dq, dq_t = r["dkv"], r["go"], r["dq"], att_t
     take, take_y, gkv = r["take"], r["take_y"], r["gkv"]
     dkv[...] = jnp.zeros(dkv.shape, BF16)
 

time: 176 us -> 175 us (level)
  no operation moved by 1% of the time
where the time goes in v1:
time: 175 us; the launch traced here: 174 us
  Pallas kernels  173 us (99%)
    pallas_call x1, Pallas kernels, block(): pl.pallas_call(block_kernel, name='block', out_shape=(jax.ShapeDtypeStruc...  168 us
    pallas_call x1, Pallas kernels, finish(): pl.pallas_call(finish_kernel, name='finish', out_shape=[jax.ShapeDtypeStr...  5.31 us

profile of v1, /device:TPU:0, one launch (start us, length us, event | category | flops | bytes accessed | tf_op | source)
XLA Modules:
  0.0 173.9 jit_solution(3626520827057887534)
XLA Ops:
  0.6 167.8 %block.1 = (bf16[320,512]{1,0:T(8,128)(2,1)}, bf16[320,512]{1,0:T(8,128)(2,1)}, bf16[320,1280]{1,0:T(8,128)(2,1)}, bf16[320,1280]{1,0:T(8,128)(2,1)}, bf16[320,6...) custom-call(bf16[320,512]{1,0:T(8,128)(2,1)} %bitcast.7, bf16[320,512]{1,0:T(8,128)(2,1)} %bitcast.8, ...), custom_call_target="tpu_custom_call" | custom-call | tf_op jit(solution)/shard_map/block/pallas_call | solution.py:1024
  168.4 5.3 %finish.1 = (bf16[320,512]{1,0:T(8,128)(2,1)}, bf16[320,512]{1,0:T(8,128)(2,1)}, f32[2,320]{1,0:T(2,128)}, f32[2,320]{1,0:T(2,128)}, f32[3,320,320]{2,1,0:T(8,12...) custom-call(bf16[320,512]{1,0:T(8,128)(2,1)} %get-tuple-element.31.r, ...), custom_call_target="tpu_custom_call" | custom-call | tf_op jit(solution)/shard_map/finish/pallas_call | solution.py:1107

commit v2 on v1

--- a/solution.py
+++ b/solution.py
@@ -41,6 +41,8 @@
 
 
 def tile_of(i, size):
+    if isinstance(i, int):
+        return slice(i * size, (i + 1) * size)
     return pl.ds(pl.multiple_of(i * size, size), size)
 
 
@@ -759,16 +761,14 @@
             links, at, grad, columns, r["pair_" + tag], r["strips_" + tag], r["cross_" + tag], final
         )
 
-    @pl.loop(0, TILES)
-    def _(t):
+    for t in range(TILES):
         grad_t[tile_of(t, 256), :] = tn(d_all[:, tile_of(t, 256)], hid[...]).astype(BF16)
 
     whole = slice(0, D)
     sum_t = gradient_sum("t", grad_t, whole, fin_t)
     sum_t.send_core()
 
-    @pl.loop(0, TILES)
-    def _(t):
+    for t in range(TILES):
         grad_f[tile_of(t, 256), :] = tn(x2[:, tile_of(t, 256)], gp[...]).astype(BF16)
 
     sum_f = GradientSumY(links, at, grad_f, r["pair_f"], r["cross_f"], r["strips_f"], r["half_f"], fin_f)
@@ -796,8 +796,7 @@
     sum_p.sent()
     sum_b = SumZ(links, at, stage, r["parts_b"], r["over_b"])
 
-    @pl.loop(0, TILES)
-    def _(t):
+    for t in range(TILES):
         product = nt(hid[...], wt[tile_of(t, 256), :]).astype(BF16)
         for i in range(4):
             stage[i, :, tile_of(t, 256)] = product[i * ROWS : (i + 1) * ROWS]
@@ -907,8 +906,7 @@
 
     sum_t.sent_core()
 
-    @pl.loop(0, TILES)
-    def _(t):
+    for t in range(TILES):
         tile = tile_of(t, 256)
         pieces = [tn(x1[:, tile], dq[...]).astype(BF16), tn(g_all[:, tile], att[...]).astype(BF16)]
         grad_t[tile, PAIR:] = jnp.concatenate(pieces, axis=1)
@@ -934,8 +932,7 @@
             gkv[rows_of(slots[j] * ROWS), tile] = total.astype(BF16)
 
 
-    @pl.loop(0, TILES)
-    def _(t):
+    for t in range(TILES):
         tile = tile_of(t, 256)
         grad_t[tile, 0:PAIR] = tn(x1[:, tile], gkv[...]).astype(BF16)
 

time: 175 us -> 187 us (1.069); the launches traced: 174 us -> 183 us
  Pallas kernels: 173 us -> 182 us
    pallas_call x1, Pallas kernels: 168 us -> 177 us  [block(): pl.pallas_call(block_kernel, name='block', out_shape=(jax.ShapeDtypeStruc...]
where the time goes in v2:
time: 187 us; the launch traced here: 183 us
  Pallas kernels  182 us (97%)
    pallas_call x1, Pallas kernels, block(): pl.pallas_call(block_kernel, name='block', out_shape=(jax.ShapeDtypeStruc...  177 us
    pallas_call x1, Pallas kernels, finish(): pl.pallas_call(finish_kernel, name='finish', out_shape=[jax.ShapeDtypeStr...  5.31 us

profile of v2, /device:TPU:0, one launch (start us, length us, event | category | flops | bytes accessed | tf_op | source)
XLA Modules:
  0.0 183.2 jit_solution(12792578735166464995)
XLA Ops:
  0.6 177.0 %block.1 = (bf16[320,512]{1,0:T(8,128)(2,1)}, bf16[320,512]{1,0:T(8,128)(2,1)}, bf16[320,1280]{1,0:T(8,128)(2,1)}, bf16[320,1280]{1,0:T(8,128)(2,1)}, bf16[320,6...) custom-call(bf16[320,512]{1,0:T(8,128)(2,1)} %bitcast.7, bf16[320,512]{1,0:T(8,128)(2,1)} %bitcast.8, ...), custom_call_target="tpu_custom_call" | custom-call | tf_op jit(solution)/shard_map/block/pallas_call | solution.py:1021
  177.7 5.3 %finish.1 = (bf16[320,512]{1,0:T(8,128)(2,1)}, bf16[320,512]{1,0:T(8,128)(2,1)}, f32[2,320]{1,0:T(2,128)}, f32[2,320]{1,0:T(2,128)}, f32[3,320,320]{2,1,0:T(8,12...) custom-call(bf16[320,512]{1,0:T(8,128)(2,1)} %get-tuple-element.31.r, ...), custom_call_target="tpu_custom_call" | custom-call | tf_op jit(solution)/shard_map/finish/pallas_call | solution.py:1104
